TPU v7x, 512 devices: a whole 4x8x8 slice. The times are simulated.
512 devices in a mesh: expert: 128 (over z, y, core), section: 4 (over x).
Axes of the slice: x: 4, y: 8, z: 8, core: 2. Of those that a mesh axis runs over, the one named last changes fastest.
Arguments:
- prev_out: bfloat16 [4, 1024, 3584], P('section', 'expert'), may hold values from -6 to 6
- next_grad: bfloat16 [4, 1024, 3584], P('section', 'expert'), may hold values from -3 to 3
- expert_ids: int32 [4, 1024, 8], P('section', 'expert'), may hold values from 0 to 15, all different within a row; in each aligned block of 8 rows (0 to 7, 8 to 15, ..., all dimensions but the last counted through in order) at most 5 rows name the same one
- affinity: float32 [4, 1024, 8], P('section', 'expert'), may hold values from 0.2 to 1
- w_gate_up: bfloat16 [4, 128, 3584, 256], P('section', 'expert'), may hold values from -0.09375 to 0.09375
- w_down: bfloat16 [4, 128, 128, 3584], P('section', 'expert'), may hold values from -0.1875 to 0.1875
Outputs:
- input_grad: bfloat16 [4, 1024, 3584], P('section', 'expert')
- grad_down: bfloat16 [4, 128, 128, 3584], P('section', 'expert')
- score_grad: float32 [4, 1024, 8], P('section', 'expert')
Inputs may be any that keep to these rules, and one draw needn't show every extreme that they name: `expert_ids`: in each section the 8 tokens of one device, each naming 8 different experts, name any one expert at most 5 times.
All inputs are finite; a program needn't handle non-finite values.
Results may differ from a plain program's by a relative error of at most 0.013.
Values may be sent and summed in bfloat16 or wider, within the bound.
A program may use at most 128 MiB of HBM per device.

v0:
```python
import jax
import jax.numpy as jnp
from jax import lax
from jax.sharding import PartitionSpec as P


def shifted(value, axis, by):
    length = lax.axis_size(axis)
    return lax.ppermute(value, axis, [(i, (i + by) % length) for i in range(length)])


def forward_rows(rows_x, w_in, units):
    gate_up = jnp.dot(rows_x, w_in, preferred_element_type=jnp.float32)
    a_part = gate_up[:, :units]
    b_part = gate_up[:, units:]
    sigmoid_a = jax.nn.sigmoid(a_part)
    active = a_part * sigmoid_a
    hidden = (active * b_part).astype(jnp.bfloat16)
    return (a_part, b_part, sigmoid_a, active, hidden)


def backward_rows(rows_g, w_in, w_out, saved):
    a_part, b_part, sigmoid_a, active, hidden = saved
    q_rows = lax.dot_general(
        rows_g, w_out, (((1,), (1,)), ((), ())), preferred_element_type=jnp.float32
    )
    r_rows = jnp.sum(hidden.astype(jnp.float32) * q_rows, axis=1).astype(jnp.bfloat16)
    grad_ab = jnp.concatenate(
        [q_rows * b_part * sigmoid_a * (1.0 + a_part * (1.0 - sigmoid_a)), q_rows * active], axis=1
    ).astype(jnp.bfloat16)
    dx_rows = lax.dot_general(
        grad_ab, w_in, (((1,), (1,)), ((), ())), preferred_element_type=jnp.float32
    ).astype(jnp.bfloat16)
    grad_dn = lax.dot_general(
        hidden, rows_g, (((0,), (0,)), ((), ())), preferred_element_type=jnp.float32
    ).astype(jnp.bfloat16)
    return (dx_rows, r_rows, grad_dn)


def on_device(prev_out, next_grad, expert_ids, affinity, w_gate_up, w_down):
    x_in = shifted(prev_out, "section", 1)[0]
    dy_in = shifted(next_grad, "section", -1)[0]
    chosen_ids = expert_ids[0]
    chosen = affinity[0]
    tok_rows, top = chosen_ids.shape
    width = x_in.shape[1]
    slices = lax.axis_size("expert")
    experts = max(top, slices // 8)
    split = slices // experts
    capacity = max(2, min(tok_rows, tok_rows * top * 5 // (4 * experts)))
    count_routes = tok_rows * top
    routes = chosen_ids.reshape(-1)
    onehot = (routes[:, None] == jnp.arange(experts, dtype=jnp.int32)[None, :]).astype(jnp.int32)
    rank = jnp.cumsum(onehot, axis=0, dtype=jnp.int32) - 1
    slot = jnp.sum(rank * onehot, axis=1, dtype=jnp.int32)
    place = routes * capacity + slot
    table = (
        jnp.full((experts * capacity,), count_routes, jnp.int32)
        .at[place]
        .set(jnp.arange(count_routes, dtype=jnp.int32))
    )
    target = jnp.repeat(table.reshape(experts, capacity), split, axis=0)
    token = target // top
    total = jnp.sum(chosen, axis=1)
    weight = chosen / total[:, None]
    scaled = (
        (weight[:, :, None] * dy_in[:, None, :].astype(jnp.float32))
        .astype(jnp.bfloat16)
        .reshape(-1, width)
    )
    x_pad = jnp.concatenate([x_in, jnp.zeros((1, width), jnp.bfloat16)], axis=0)
    g_pad = jnp.concatenate([scaled, jnp.zeros((1, width), jnp.bfloat16)], axis=0)
    send_x = x_pad[token]
    send_g = g_pad[target]
    w_in = w_gate_up[0, 0]
    w_out = w_down[0, 0]
    units = w_out.shape[0]
    got_x, got_g = (
        lax.all_to_all(send_x, "expert", split_axis=0, concat_axis=0, tiled=True),
        lax.all_to_all(send_g, "expert", split_axis=0, concat_axis=0, tiled=True),
    )
    rows_x = got_x.reshape(-1, width)
    saved = forward_rows(rows_x, w_in, units)
    rows_g = got_g.reshape(-1, width)
    dx_rows, r_rows, grad_dn = backward_rows(rows_g, w_in, w_out, saved)
    back_x, back_r = (
        lax.all_to_all(
            dx_rows.reshape(slices, capacity, width),
            "expert",
            split_axis=0,
            concat_axis=0,
            tiled=True,
        ),
        lax.all_to_all(
            r_rows.reshape(slices, capacity), "expert", split_axis=0, concat_axis=0, tiled=True
        ),
    )
    flat_x = back_x.reshape(-1, width)
    flat_r = back_r.reshape(-1).astype(jnp.float32)
    input_sum = (
        jnp.zeros((tok_rows + 1, width), jnp.float32)
        .at[token.reshape(-1)]
        .add(flat_x.astype(jnp.float32))[:tok_rows]
    )
    r_flat = (
        jnp.zeros((count_routes + 1,), jnp.float32)
        .at[target.reshape(-1)]
        .add(flat_r)[:count_routes]
    )
    input_grad = input_sum.astype(jnp.bfloat16)
    r_val = r_flat.reshape(tok_rows, top)
    score_grad = r_val / chosen - jnp.sum(r_val, axis=1, keepdims=True) / total[:, None]
    return (input_grad[None], grad_dn[None, None], score_grad[None])


def solution(mesh):
    in_specs = (
        P("section", "expert", None),
        P("section", "expert", None),
        P("section", "expert", None),
        P("section", "expert", None),
        P("section", "expert", None, None),
        P("section", "expert", None, None),
    )
    out_specs = (
        P("section", "expert", None),
        P("section", "expert", None, None),
        P("section", "expert", None),
    )
    return jax.shard_map(
        on_device, mesh=mesh, in_specs=in_specs, out_specs=out_specs, check_vma=False
    )
```

profile of v0, /device:TPU:152, one launch (start us, length us, event | category | flops | bytes accessed | tf_op | source)
XLA Modules:
  0.0 791.4 jit_solution(14999780269286103956)
XLA Ops:
  0.6 3.5 collective-permute-start.1
  4.2 0.8 eq.15
  5.0 0.7 broadcast_multiply_fusion
  6.1 0.8 scatter_custom_fusion
  7.2 1.0 collective-permute-done.1
  8.3 5.1 gather_fusion.1
  13.4 7.8 reshape.347
  21.2 16.0 %all-to-all-start.1 = ((bf16[128,5,3584]{2,1,0:T(8,128)(2,1)}), bf16[128,5,3584]{2,1,0:T(8,128)(2,1)}, u32[]{:S(2)}, u32[]{:S(2)}) async-start(bf16[128,5,3584]{2,1,0:T(8,128)(2,1)} %reshape.347), calls=%async_computation.1 | async-start | bytes 14680064 | tf_op jit(solution)/shard_map/all_to_all | solution.py:79
  37.2 3.5 collective-permute-start
  41.3 2.0 collective-permute-done
  43.5 5.2 gather_fusion
  48.7 7.8 reshape.339
  56.5 201.4 %all-to-all-done.1 = bf16[128,5,3584]{2,1,0:T(8,128)(2,1)} async-done(((bf16[128,5,3584]{2,1,0:T(8,128)(2,1)}), bf16[128,5,3584]{2,1,0:T(8,128)(2,1)}, u32[]{:S(2)}, u32[]{:S(2)}) %all-to-all-start.1) | async-done | bytes 4587552 | tf_op jit(solution)/shard_map/all_to_all | solution.py:79
  257.9 9.9 %all-to-all-start = ((bf16[128,5,3584]{2,1,0:T(8,128)(2,1)}), bf16[128,5,3584]{2,1,0:T(8,128)(2,1)}, u32[]{:S(2)}, u32[]{:S(2)}) async-start(bf16[128,5,3584]{2,1,0:T(8,128)(2,1)} %reshape.339), calls=%async_computation | async-start | bytes 14680064 | tf_op jit(solution)/shard_map/all_to_all | solution.py:80
  267.8 8.1 %reshape.331 = bf16[640,3584]{1,0:T(8,128)(2,1)} reshape(bf16[128,5,3584]{2,1,0:T(8,128)(2,1)} %all-to-all-done.1) | data formatting | bytes 9175040 | tf_op jit(solution)/shard_map/reshape | solution.py:82
  275.9 4.8 fusion.2
  280.6 207.8 %all-to-all-done = bf16[128,5,3584]{2,1,0:T(8,128)(2,1)} async-done(((bf16[128,5,3584]{2,1,0:T(8,128)(2,1)}), bf16[128,5,3584]{2,1,0:T(8,128)(2,1)}, u32[]{:S(2)}, u32[]{:S(2)}) %all-to-all-start) | async-done | bytes 4587552 | tf_op jit(solution)/shard_map/all_to_all | solution.py:80
  488.4 8.1 %reshape.330 = bf16[640,3584]{1,0:T(8,128)(2,1)} reshape(bf16[128,5,3584]{2,1,0:T(8,128)(2,1)} %all-to-all-done) | data formatting | bytes 9175040 | tf_op jit(solution)/shard_map/reshape | solution.py:84
  496.5 4.0 multiply_reduce_fusion
  500.5 0.9 convert_element_type.75
  501.4 9.6 %all-to-all-start.3 = ((bf16[128,1,5]{2,1,0:T(2,128)(2,1)}), bf16[128,1,5]{2,1,0:T(2,128)(2,1)S(1)}, u32[]{:S(2)}, u32[]{:S(2)}) async-start(bf16[128,1,5]{2,1,0:T(2,128)(2,1)} %convert_element_type.75), calls=%async_computation.3 | async-start | bytes 131072 | tf_op jit(solution)/shard_map/all_to_all | solution.py:94
  511.0 3.6 convolution_convert_fusion
  514.6 7.9 reshape.332
  522.5 14.1 %all-to-all-start.2 = ((bf16[128,5,3584]{2,1,0:T(8,128)(2,1)}), bf16[128,5,3584]{2,1,0:T(8,128)(2,1)}, u32[]{:S(2)}, u32[]{:S(2)}) async-start(bf16[128,5,3584]{2,1,0:T(8,128)(2,1)} %reshape.332), calls=%async_computation.2 | async-start | bytes 14680064 | tf_op jit(solution)/shard_map/all_to_all | solution.py:87
  536.7 0.2 reshape.328
  536.9 4.1 fusion
  541.4 5.9 scatter_custom_fusion.2
  547.6 0.7 divide_subtract_fusion
  548.2 209.1 %all-to-all-done.2 = bf16[128,5,3584]{2,1,0:T(8,128)(2,1)} async-done(((bf16[128,5,3584]{2,1,0:T(8,128)(2,1)}), bf16[128,5,3584]{2,1,0:T(8,128)(2,1)}, u32[]{:S(2)}, u32[]{:S(2)}) %all-to-all-start.2) | async-done | bytes 4587552 | tf_op jit(solution)/shard_map/all_to_all | solution.py:87
  757.3 9.2 %reshape.366 = f32[640,3584]{1,0:T(8,128)} reshape(bf16[128,5,3584]{2,1,0:T(8,128)(2,1)} %all-to-all-done.2) | data formatting | bytes 13762560 | tf_op jit(solution)/shard_map/convert_element_type | solution.py:103
  766.5 24.3 %scatter_custom_fusion.1 = f32[9,3584]{1,0:T(8,128)S(1)} fusion(s32[640]{0:T(1024)S(1)} %get-tuple-element.4, f32[640,3584]{1,0:T(8,128)} %reshape.366, f32[]{:T(128)} %constant.13.clone.1), kind=kCustom, calls=%fused_computation.34 | custom fusion | flops 2293760 | bytes 129536 | tf_op jit(solution)/shard_map/scatter-add | solution.py:103
  790.8 0.6 fusion.20
  (38 shorter events, 2.2 us)
Async XLA Ops:
  0.6 275.2 %copy-start = (bf16[1,1,3584,256]{3,2,1,0:T(8,128)(2,1)S(1)}, bf16[1,1,3584,256]{3,2,1,0:T(8,128)(2,1)}, u32[]{:S(2)}) copy-start(bf16[1,1,3584,256]{3,2,1,0:T(8,128)(2,1)} %param.10) | copy-start | bytes 5505028
  0.6 7.6 collective-permute-start.1
  21.2 16.0 %copy-start.3 = (bf16[1,8,3584]{2,1,0:T(8,128)(2,1)S(1)}, bf16[1,8,3584]{2,1,0:T(8,128)(2,1)}, u32[]{:S(2)}) copy-start(bf16[1,8,3584]{2,1,0:T(8,128)(2,1)} %param.7) | copy-start | bytes 172036
  21.2 19.5 %copy-start.1 = (f32[1,8,8]{2,1,0:T(8,128)S(1)}, f32[1,8,8]{2,1,0:T(8,128)}, u32[]{:S(2)}) copy-start(f32[1,8,8]{2,1,0:T(8,128)} %param.9) | copy-start | bytes 772
  21.2 236.7 %all-to-all-start.1 = ((bf16[128,5,3584]{2,1,0:T(8,128)(2,1)}), bf16[128,5,3584]{2,1,0:T(8,128)(2,1)}, u32[]{:S(2)}, u32[]{:S(2)}) async-start(bf16[128,5,3584]{2,1,0:T(8,128)(2,1)} %reshape.347), calls=%async_computation.1 | async-start | bytes 14680064 | tf_op jit(solution)/shard_map/all_to_all | solution.py:79
  37.2 6.1 collective-permute-start
  257.9 230.6 %all-to-all-start = ((bf16[128,5,3584]{2,1,0:T(8,128)(2,1)}), bf16[128,5,3584]{2,1,0:T(8,128)(2,1)}, u32[]{:S(2)}, u32[]{:S(2)}) async-start(bf16[128,5,3584]{2,1,0:T(8,128)(2,1)} %reshape.339), calls=%async_computation | async-start | bytes 14680064 | tf_op jit(solution)/shard_map/all_to_all | solution.py:80
  280.6 215.9 %copy-start.2 = (bf16[1,1,128,3584]{3,2,1,0:T(8,128)(2,1)S(1)}, bf16[1,1,128,3584]{3,2,1,0:T(8,128)(2,1)}, u32[]{:S(2)}) copy-start(bf16[1,1,128,3584]{3,2,1,0:T(8,128)(2,1)} %param.11) | copy-start | bytes 2752516
  501.4 21.1 %all-to-all-start.3 = ((bf16[128,1,5]{2,1,0:T(2,128)(2,1)}), bf16[128,1,5]{2,1,0:T(2,128)(2,1)S(1)}, u32[]{:S(2)}, u32[]{:S(2)}) async-start(bf16[128,1,5]{2,1,0:T(2,128)(2,1)} %convert_element_type.75), calls=%async_computation.3 | async-start | bytes 131072 | tf_op jit(solution)/shard_map/all_to_all | solution.py:94
  522.5 234.8 %all-to-all-start.2 = ((bf16[128,5,3584]{2,1,0:T(8,128)(2,1)}), bf16[128,5,3584]{2,1,0:T(8,128)(2,1)}, u32[]{:S(2)}, u32[]{:S(2)}) async-start(bf16[128,5,3584]{2,1,0:T(8,128)(2,1)} %reshape.332), calls=%async_computation.2 | async-start | bytes 14680064 | tf_op jit(solution)/shard_map/all_to_all | solution.py:87
where the time goes:
time: 793 us; the launch traced here: 791 us
  waiting for transfers between devices  621 us (78%)
  local copies, waits for them, and re-layouts  63.7 us (8%)
  starting transfers between devices  56.6 us (7%)
  other arithmetic  32.5 us (4%)
  matrix products  16.4 us (2%)
    all_to_all x1, waiting for transfers between devices, on_device(): lax.all_to_all(dx_rows.reshape(slices, capacity, width), 'expert', split_...  209 us
    all_to_all x1, waiting for transfers between devices, on_device(): lax.all_to_all(send_g, 'expert', split_axis=0, concat_axis=0, tiled=True)  208 us
    all_to_all x1, waiting for transfers between devices, on_device(): lax.all_to_all(send_x, 'expert', split_axis=0, concat_axis=0, tiled=True)  201 us
    scatter-add x1, other arithmetic, on_device(): input_sum = jnp.zeros((tok_rows + 1, width), jnp.float32).at[token.reshap...  24.3 us
    all_to_all x1, starting transfers between devices, on_device(): lax.all_to_all(send_x, 'expert', split_axis=0, concat_axis=0, tiled=True)  16 us
  transfers between devices with their start and end apart: 6, of which 5 were waited for; matrix products, arithmetic and copies ran while one was open for 7% of the time, Pallas kernels for 0%

commit v1 on v0

v1 whole, which is shorter than its diff:
```python
import functools

import jax
import jax.numpy as jnp
from jax import lax
from jax.experimental import pallas as pl
from jax.experimental.pallas import tpu as pltpu
from jax.sharding import PartitionSpec as P

MESH = pl.DeviceIdType.MESH
F32 = jnp.float32
BF16 = jnp.bfloat16
LANES = 128
VMEM_BYTES = 60 * 1024 * 1024


def wrap(value, length):
    return lax.rem(value + length, length)


def order_of(index, length):
    if isinstance(index, int):
        return (length - index) // 2, 1 - 2 * (index % 2)
    return lax.div(length - index, 2), 1 - 2 * lax.rem(index, 2)


def place(index, centre, length):
    hops, sign = order_of(index, length)
    return wrap(centre + sign * hops, length)


def kernel(
    R,
    sections,
    split,
    x_ref,
    g_ref,
    ids_ref,
    aff_ref,
    win_hbm,
    wout_hbm,
    dx_out,
    gd_out,
    sg_out,
    buf,
    win,
    wout,
    shift_src,
    shift_dst,
    wt_src,
    wt_dst,
    ab,
    qb,
    gab,
    hw,
    rb,
    acc,
    pair_src,
    pair_dst,
    ring_src,
    ring_dst,
    line_src,
    line_dst,
    fin_src,
    fin_dst,
    load_sem,
    shift_send,
    shift_recv,
    wt_sem,
    a_send,
    a_recv,
    b_send,
    b_recv,
    sib_send,
    sib_recv,
    pair_send,
    pair_recv,
    ring_send,
    ring_recv,
    line_send,
    line_recv,
    fin_sem,
):
    half = R // 2
    rows, D = x_ref.shape
    H = D // 2
    block = 2 * rows
    units = wout.shape[0]
    top = ids_ref.shape[1]
    per = ring_src.shape[3]
    groups = R // per
    me = lax.axis_index("expert")
    sec = lax.axis_index("section")
    c = lax.rem(me, 2)
    chip = lax.div(me, 2)
    z, y = lax.div(chip, R), lax.rem(chip, R)
    a = y + c * (z - y)
    b = z + c * (y - z)
    expert = lax.div(me, split)
    sec_next, sec_prev = wrap(sec + 1, sections), wrap(sec - 1, sections)

    def at(a_pos, b_pos):
        z_pos = b_pos + c * (a_pos - b_pos)
        y_pos = a_pos + c * (b_pos - a_pos)
        return {"expert": (z_pos * R + y_pos) * 2 + c, "section": sec}

    a_next, a_prev = at(wrap(a + 1, R), b), at(wrap(a - 1, R), b)
    b_next, b_prev = at(a, wrap(b + 1, R)), at(a, wrap(b - 1, R))
    sibling = {"expert": chip * 2 + 1 - c, "section": sec}

    def remote(src, dst, send, recv, device):
        return pltpu.make_async_remote_copy(
            src_ref=src, dst_ref=dst, send_sem=send, recv_sem=recv, device_id=device, device_id_type=MESH
        )

    load_in = pltpu.make_async_copy(win_hbm, win, load_sem.at[0])
    load_out = pltpu.make_async_copy(wout_hbm, wout, load_sem.at[1])
    load_in.start()
    load_out.start()

    barrier = pltpu.get_barrier_semaphore()
    source = wrap(sec - 1 + 2 * c, sections)
    for device in (
        a_next,
        a_prev,
        b_next,
        b_prev,
        sibling,
        {"expert": chip * 2, "section": source},
        {"expert": chip * 2 + 1, "section": source},
    ):
        pl.semaphore_signal(barrier, inc=1, device_id=device, device_id_type=MESH)

    def packed(value):
        wide = value.astype(F32)
        return jnp.concatenate([wide[:, :H], wide[:, H:]], axis=0).astype(BF16)

    shift_src[0] = packed(x_ref[...])
    shift_src[1] = packed(g_ref[...])
    chosen = aff_ref[...]
    ids = ids_ref[...]
    total = jnp.sum(chosen, axis=1, keepdims=True)
    weight = chosen / total
    lane8 = lax.broadcasted_iota(jnp.int32, (rows, LANES), 1)
    dense = jnp.zeros((rows, LANES), F32)
    for k in range(top):
        dense = dense + jnp.where(lane8 == ids[:, k : k + 1], weight[:, k : k + 1], 0.0)
    wt_src[...] = dense
    pl.semaphore_wait(barrier, 7)

    send_x = remote(
        shift_src.at[0], shift_dst.at[c], shift_send.at[0], shift_recv.at[c], {"expert": chip * 2, "section": sec_next}
    )
    send_g = remote(
        shift_src.at[1], shift_dst.at[c], shift_send.at[1], shift_recv.at[c], {"expert": chip * 2 + 1, "section": sec_prev}
    )
    send_w = remote(wt_src, wt_dst, wt_sem.at[0], wt_sem.at[1], sibling)
    send_x.start()
    send_g.start()
    send_w.start()
    for i in range(2):
        remote(shift_src.at[0], shift_dst.at[i], shift_send.at[0], shift_recv.at[i], sibling).wait_recv()
    send_w.wait_recv()
    low, high = shift_dst[0].astype(F32), shift_dst[1].astype(F32)
    mine, other = wt_src[...], wt_dst[...]
    pair_wt = jnp.concatenate([jnp.where(c == 0, mine, other), jnp.where(c == 0, other, mine)], axis=0)
    lead = pair_wt.astype(BF16).astype(F32)
    buf[c, b, a, :, 0:H] = jnp.concatenate([low[:rows], high[:rows]], axis=0).astype(BF16)
    buf[c, b, a, :, H:D] = jnp.concatenate([low[rows:], high[rows:]], axis=0).astype(BF16)
    buf[c, b, a, :, D:] = jnp.where(c == 0, lead, pair_wt - lead).astype(BF16)

    def along_a(j, way, hop):
        return remote(
            buf.at[c, b, j], buf.at[c, b, j], a_send.at[way, hop], a_recv.at[way, hop], a_next if way == 0 else a_prev
        )

    def along_b(origin, j, way, hop, piece):
        return remote(
            buf.at[c, origin, j],
            buf.at[c, origin, j],
            b_send.at[way, hop],
            b_recv.at[way, hop, piece],
            b_next if way == 0 else b_prev,
        )

    def to_sibling(origin, j):
        return remote(buf.at[c, origin, j], buf.at[c, origin, j], sib_send.at[origin], sib_recv.at[origin], sibling)

    for o in range(R):
        hops, sign = order_of(R - 1 - o, R)
        j = wrap(a + sign * hops, R)
        if o == 0:
            if half > 1:
                along_a(j, 0, 1).start()
            along_a(j, 1, 1).start()
        elif sign > 0:
            along_a(j, 1, hops).wait_recv()
            if hops < half:
                along_a(j, 1, hops + 1).start()
        else:
            along_a(j, 0, hops).wait_recv()
            if hops < half - 1:
                along_a(j, 0, hops + 1).start()
        if half > 1 or o < half:
            along_b(b, j, 0, 1, o).start()
        if half > 1 or o >= half:
            along_b(b, j, 1, 1, o).start()
        to_sibling(b, j).start()

    def forward(hop, o, carry):
        j = place(R - 1 - o, a, R)
        left, right = wrap(b - (hop - 1), R), wrap(b + (hop - 1), R)
        along_b(left, j, 0, hop - 1, o).wait_recv()
        if hop < half:
            along_b(left, j, 0, hop, o).start()
        else:

            @pl.when(o < half)
            def _():
                along_b(left, j, 0, hop, o).start()

        to_sibling(left, j).start()
        along_b(right, j, 1, hop - 1, o).wait_recv()
        if hop < half:
            along_b(right, j, 1, hop, o).start()
        else:

            @pl.when(o >= half)
            def _():
                along_b(right, j, 1, hop, o).start()

        to_sibling(right, j).start()
        return carry

    def wait_sibling(origin):
        remote(buf.at[1 - c, origin], buf.at[1 - c, origin], sib_send.at[origin], sib_recv.at[origin], sibling).wait_recv()

    def project(z_slab, y_slab):
        rows_lo = buf[0, z_slab, :, :, 0:H].reshape(R * block, H)
        rows_hi = buf[0, z_slab, :, :, H:D].reshape(R * block, H)
        ab[z_slab] = jnp.dot(rows_lo, win[0], preferred_element_type=F32) + jnp.dot(
            rows_hi, win[1], preferred_element_type=F32
        )
        rows_g = buf[1, y_slab, :, :, 0:D].reshape(R * block, D)
        q = lax.dot_general(rows_g, wout[...], (((1,), (1,)), ((), ())), preferred_element_type=F32)
        qb[:, y_slab] = q.reshape(R, block, units)

    def project_at(distance):
        if distance == 0 or distance == half:
            wait_sibling(wrap(a + distance, R))
            project(wrap(z + distance, R), wrap(y + distance, R))
        else:

            def side(i, carry):
                step = distance * (1 - 2 * i)
                wait_sibling(wrap(a + step, R))
                project(wrap(z + step, R), wrap(y + step, R))
                return carry

            lax.fori_loop(0, 2, side, 0)

    for hop in range(2, half + 1):
        lax.fori_loop(0, R, functools.partial(forward, hop), 0)
        if hop == 2:
            load_in.wait()
            load_out.wait()
        project_at(hop - 2)
    if half == 1:
        load_in.wait()
        load_out.wait()
    project_at(half - 1)
    far = wrap(b + half, R)

    def last(o, carry):
        j = place(R - 1 - o, a, R)
        along_b(far, j, 0, half, o).wait_recv()
        to_sibling(far, j).start()
        j = place(R - 1 - (o + half), a, R)
        along_b(far, j, 1, half, o + half).wait_recv()
        to_sibling(far, j).start()
        return carry

    lax.fori_loop(0, half, last, 0)
    project_at(half)

    def activate(z_slab, carry):
        lane = lax.broadcasted_iota(jnp.int32, (R * block, LANES), 1)
        wt = buf[0, z_slab, :, :, D:].astype(F32) + buf[1, :, z_slab, :, D:].astype(F32)
        w = jnp.sum(jnp.where(lane == expert, wt.reshape(R * block, LANES), 0.0), axis=1, keepdims=True)
        a_part = ab[z_slab, :, 0:units]
        b_part = ab[z_slab, :, units:]
        q = qb[z_slab].reshape(R * block, units) * w
        sig = jax.nn.sigmoid(a_part)
        active = a_part * sig
        hidden = active * b_part
        r = jnp.sum(hidden.astype(BF16).astype(F32) * q, axis=1, keepdims=True)
        gab[z_slab, :, :, 0:units] = (
            (q * b_part * sig * (1.0 + a_part * (1.0 - sig))).astype(BF16).reshape(R, block, units)
        )
        gab[z_slab, :, :, units:] = (q * active).astype(BF16).reshape(R, block, units)
        hw[:, z_slab] = (hidden * w).astype(BF16).reshape(R, block, units)
        rb[z_slab] = jnp.where(lane == expert, r, 0.0).astype(BF16).reshape(R, block, LANES)
        return carry

    lax.fori_loop(0, R, activate, 0)

    def spot(target, j, swap):
        return target + swap * (j - target), j + swap * (target - j)

    def products(target, centre, swap, h):
        parts = []
        for u in range(R):
            zi, yi = spot(target, place(u, centre, R), swap)
            parts.append(gab[zi, yi])
        rows_ab = jnp.concatenate(parts, axis=0)
        return lax.dot_general(rows_ab, win[h], (((1,), (1,)), ((), ())), preferred_element_type=F32)

    def pair_copy(n):
        return remote(pair_src.at[n], pair_dst.at[n], pair_send.at[n], pair_recv.at[n], sibling)

    def give(n):
        value = products(place(n, a, R), b, 1 - c, 1 - c)
        pair_src[n] = value.astype(BF16).reshape(R, block, H)
        pair_copy(n).start()

    def ring_copy(way, hop, g):
        return remote(
            ring_src.at[way, hop, g],
            ring_dst.at[way, hop, g],
            ring_send.at[way, hop],
            ring_recv.at[way, hop, g],
            b_next if way == 0 else b_prev,
        )

    def wait_ring(way, hop, g):
        ring_copy(way, hop, g).wait_recv()

    def dense_r(target, g):
        parts = []
        for i in range(per):
            zi, yi = spot(target, place(g * per + i, a, R), c)
            parts.append(rb[zi, yi].astype(F32)[None])
        return jnp.concatenate(parts, axis=0)

    def keep(n):
        acc[...] = products(place(n, b, R), a, c, c).reshape(groups, per, block, H)
        pair_copy(n).wait_recv()

    def local_sum(n, g):
        value = acc[g] + pair_dst[n, pl.ds(g * per, per)].astype(F32)
        return value, dense_r(place(n, b, R), g)

    def send_on(way, hop, g, value, r_value):
        ring_src[way, hop, g, :, :, 0:H] = value.astype(BF16)
        ring_src[way, hop, g, :, :, H:] = r_value.astype(BF16)

    def start_ring(hop, g, sign):
        @pl.when(sign > 0)
        def _():
            ring_copy(0, hop, g).start()

        @pl.when(sign < 0)
        def _():
            ring_copy(1, hop, g).start()

    give(0)
    if R > 1:
        give(1)

    keep(0)
    give(min(2, R - 1)) if R > 2 else None
    for g in range(groups):
        way = 0 if g < groups // 2 else 1
        value, r_value = local_sum(0, g)
        send_on(way, half, g, value, r_value)
        ring_copy(way, half, g).start()

    def relay(partial, n, carry):
        hops, sign = order_of(n, R)
        way = lax.rem(n, 2)
        keep(n)

        @pl.when(n + 2 < R)
        def _():
            give(n + 2)

        def group(g, carry):
            value, r_value = local_sum(n, g)

            def with_arrived():
                back = ring_dst.at[way, hops + 1, g]
                remote(
                    back, back, ring_send.at[way, hops + 1], ring_recv.at[way, hops + 1, g], sibling
                ).wait_recv()
                arrived = back[...].astype(F32)
                send_on(way, hops, g, value + arrived[:, :, 0:H], r_value + arrived[:, :, H:])

            if partial:
                here = lax.div(g, groups // 2) == way

                @pl.when(here)
                def _():
                    with_arrived()

                @pl.when(jnp.logical_not(here))
                def _():
                    send_on(way, hops, g, value, r_value)

            else:
                with_arrived()
            start_ring(hops, g, sign)
            return carry

        lax.fori_loop(0, groups, group, 0)
        return carry

    if R > 2:
        lax.fori_loop(1, 3, functools.partial(relay, True), 0)
    if R > 4:
        lax.fori_loop(3, R - 1, functools.partial(relay, False), 0)

    def line_copy(way, hop):
        return remote(
            line_src.at[way, hop],
            line_dst.at[way, hop],
            line_send.at[way, hop],
            line_recv.at[way, hop],
            a_next if way == 0 else a_prev,
        )

    chunk = D // 7 if D % (7 * LANES) == 0 else LANES
    chunks = D // chunk

    def grad_down(i):
        cols = pl.ds(pl.multiple_of(i * chunk, chunk), chunk)
        g_rows = buf[1, :, :, :, cols].reshape(R * R * block, chunk)
        h_rows = hw[...].reshape(R * R * block, units)
        gd_out[:, cols] = lax.dot_general(
            h_rows, g_rows, (((0,), (0,)), ((), ())), preferred_element_type=F32
        ).astype(BF16)

    n = R - 1
    keep(n)
    done = 0
    for g in range(groups):
        value, r_value = local_sum(n, g)
        for way in range(2):
            if half > 1 or (g < groups // 2) == (way == 0):
                wait_ring(way, 1, g)
                arrived = ring_dst[way, 1, g].astype(F32)
                value = value + arrived[:, :, 0:H]
                r_value = r_value + arrived[:, :, H:]
        for i in range(per):
            u = g * per + i
            hops, sign = order_of(u, R)
            v, rv = value[i], r_value[i]
            while done < chunks and done < (u + 1) * chunks // R:
                grad_down(done)
                done += 1
            ways = (0, 1) if hops == 0 else ((0,) if sign > 0 else (1,))
            for way in ways:
                if hops + 1 <= (half if way == 0 else half - 1):
                    line_copy(way, hops + 1).wait_recv()
                    arrived = line_dst[way, hops + 1].astype(F32)
                    v = v + arrived[:, 0:H]
                    rv = rv + arrived[:, H:]
            if hops > 0:
                way = ways[0]
                line_src[way, hops, :, 0:H] = v.astype(BF16)
                line_src[way, hops, :, H:] = rv.astype(BF16)
                line_copy(way, hops).start()
            else:
                fin_src[:, 0:H] = jnp.where(c == 0, v[rows:], v[:rows])
                fin_src[:, H:] = jnp.where(c == 0, rv[rows:], rv[:rows])
                swap_rows = remote(fin_src, fin_dst, fin_sem.at[0], fin_sem.at[1], sibling)
                swap_rows.start()
                own_rows = jnp.where(c == 0, v[:rows], v[rows:])
                own_r = jnp.where(c == 0, rv[:rows], rv[rows:])
                swap_rows.wait_recv()
                their_rows = fin_dst[:, 0:H]
                r_all = own_r + fin_dst[:, H:]
                dx_out[:, 0:H] = jnp.where(c == 0, own_rows, their_rows).astype(BF16)
                dx_out[:, H:] = jnp.where(c == 0, their_rows, own_rows).astype(BF16)
                swap_rows.wait_send()

    column = lax.broadcasted_iota(jnp.int32, (rows, top), 1)
    r_val = jnp.zeros((rows, top), F32)
    for k in range(top):
        r_k = jnp.sum(jnp.where(lane8 == ids[:, k : k + 1], r_all, 0.0), axis=1, keepdims=True)
        r_val = r_val + jnp.where(column == k, r_k, 0.0)
    sg_out[...] = r_val / chosen - jnp.sum(r_val, axis=1, keepdims=True) / total

    send_x.wait_send()
    send_g.wait_send()
    send_w.wait_send()
    for hop in range(1, half + 1):
        if hop < half:
            along_a(a, 0, hop).wait_send()
        along_a(a, 1, hop).wait_send()
        for way in range(2):
            count = R if hop < half else half
            slab = buf.at[c, b, pl.ds(0, count)]
            remote(slab, slab, b_send.at[way, hop], b_recv.at[way, hop, 0], sibling).wait_send()
            parts = groups if hop < half else groups // 2
            sent = ring_src.at[way, hop, pl.ds(0, parts)]
            remote(sent, sent, ring_send.at[way, hop], ring_recv.at[way, hop, 0], sibling).wait_send()
        line_copy(0, hop).wait_send()
        if hop < half:
            line_copy(1, hop).wait_send()

    def settle(i, carry):
        remote(buf.at[c, i], buf.at[c, i], sib_send.at[i], sib_recv.at[i], sibling).wait_send()
        pair_copy(i).wait_send()
        return carry

    lax.fori_loop(0, R, settle, 0)


def side_of(devices):
    R = 1
    while 2 * R * R < devices:
        R += 1
    return R


def on_device(prev_out, next_grad, expert_ids, affinity, w_gate_up, w_down):
    slices = lax.axis_size("expert")
    sections = lax.axis_size("section")
    R = side_of(slices)
    rows, D = prev_out.shape[1:]
    top = expert_ids.shape[2]
    units = w_down.shape[2]
    H = D // 2
    block = 2 * rows
    split = slices // max(top, slices // 8)
    half = R // 2
    per = max(1, R // 4)
    groups = R // per
    vmem = pl.BlockSpec(memory_space=pltpu.VMEM)
    anywhere = pl.BlockSpec(memory_space=pl.ANY)
    dma = pltpu.SemaphoreType.DMA
    flops = 2 * slices * rows * D * units * 6
    dx, gd, sg = pl.pallas_call(
        functools.partial(kernel, R, sections, split),
        out_shape=(
            jax.ShapeDtypeStruct((rows, D), BF16),
            jax.ShapeDtypeStruct((units, D), BF16),
            jax.ShapeDtypeStruct((rows, top), F32),
        ),
        in_specs=[vmem, vmem, vmem, vmem, anywhere, anywhere],
        out_specs=(vmem, vmem, vmem),
        scratch_shapes=[
            pltpu.VMEM((2, R, R, block, D + LANES), BF16),
            pltpu.VMEM((2, H, 2 * units), BF16),
            pltpu.VMEM((units, D), BF16),
            pltpu.VMEM((2, block, H), BF16),
            pltpu.VMEM((2, block, H), BF16),
            pltpu.VMEM((rows, LANES), F32),
            pltpu.VMEM((rows, LANES), F32),
            pltpu.VMEM((R, R * block, 2 * units), F32),
            pltpu.VMEM((R, R, block, units), F32),
            pltpu.VMEM((R, R, block, 2 * units), BF16),
            pltpu.VMEM((R, R, block, units), BF16),
            pltpu.VMEM((R, R, block, LANES), BF16),
            pltpu.VMEM((groups, per, block, H), F32),
            pltpu.VMEM((R, R, block, H), BF16),
            pltpu.VMEM((R, R, block, H), BF16),
            pltpu.VMEM((2, half + 1, groups, per, block, H + LANES), BF16),
            pltpu.VMEM((2, half + 1, groups, per, block, H + LANES), BF16),
            pltpu.VMEM((2, half + 1, block, H + LANES), BF16),
            pltpu.VMEM((2, half + 1, block, H + LANES), BF16),
            pltpu.VMEM((rows, H + LANES), F32),
            pltpu.VMEM((rows, H + LANES), F32),
            dma((2,)),
            dma((2,)),
            dma((2,)),
            dma((2,)),
            dma((2, half + 1)),
            dma((2, half + 1)),
            dma((2, half + 1)),
            dma((2, half + 1, R)),
            dma((R,)),
            dma((R,)),
            dma((R,)),
            dma((R,)),
            dma((2, half + 1)),
            dma((2, half + 1, groups)),
            dma((2, half + 1)),
            dma((2, half + 1)),
            dma((2,)),
        ],
        compiler_params=pltpu.CompilerParams(
            collective_id=0, has_side_effects=True, vmem_limit_bytes=VMEM_BYTES
        ),
        cost_estimate=pl.CostEstimate(flops=flops, bytes_accessed=4 * D * units * 2, transcendentals=0),
    )(
        prev_out[0],
        next_grad[0],
        expert_ids[0],
        affinity[0],
        w_gate_up[0, 0].reshape(2, H, 2 * units),
        w_down[0, 0],
    )
    return dx[None], gd[None, None], sg[None]


def solution(mesh):
    in_specs = (
        P("section", "expert", None),
        P("section", "expert", None),
        P("section", "expert", None),
        P("section", "expert", None),
        P("section", "expert", None, None),
        P("section", "expert", None, None),
    )
    out_specs = (
        P("section", "expert", None),
        P("section", "expert", None, None),
        P("section", "expert", None),
    )
    return jax.shard_map(
        on_device, mesh=mesh, in_specs=in_specs, out_specs=out_specs, check_vma=False
    )
```

time: 793 us -> 120 us (0.15)
  the two profiles are of different devices: /device:TPU:152 before, /device:TPU:1 now
where the time goes in v1:
time: 120 us
  Pallas kernels  115 us (96%)
  local copies, waits for them, and re-layouts  4.2 us (4%)
    pallas_call x1, Pallas kernels, on_device(): pl.pallas_call(functools.partial(kernel, R, sections, split), out_shape=(...  115 us
    unnamed x5, local copies, waits for them, and re-layouts  4.2 us

profile of v1, /device:TPU:1, one launch (start us, length us, event | category | flops | bytes accessed | tf_op | source)
XLA Modules:
  0.0 119.9 jit_solution(5292883425014496718)
XLA Ops:
  0.6 115.0 %shard_map.85 = (bf16[8,3584]{1,0:T(8,128)(2,1)}, bf16[128,3584]{1,0:T(8,128)(2,1)}, f32[8,8]{1,0:T(8,128)}) custom-call(bf16[8,3584]{1,0:T(8,128)(2,1)} %bitcast.14, bf16[8,3584]{1,0:T(8,128)(2,1)} %bitcast.15, s32[8,8]{1,0:T(8,128)} %bitcast.16, f32[8,8]{1,0:T(8,128)} %bitcast.17, bf16[2,1792,256]{2,1,0:T(8,128)(2,1)} %bitcast.12, bf16[128,3584]{1,0:T(8,128)(2,1)} %bitcast.13), custom_call_target="tpu_custom_call" | custom-call | flops 5637144576 | bytes 3670016 | tf_op jit(solution)/shard_map/pallas_call | solution.py:543
  115.7 0.0 copy-start
  115.7 1.4 %copy.12 = bf16[1,8,3584]{2,1,0:T(8,128)(2,1)} copy(bf16[1,8,3584]{2,1,0:T(8,128)(2,1)} %bitcast.10) | data formatting | bytes 114688
  117.1 2.2 %copy.13 = bf16[1,1,128,3584]{3,2,1,0:T(8,128)(2,1)} copy(bf16[1,1,128,3584]{3,2,1,0:T(8,128)(2,1)} %bitcast.9) | data formatting | bytes 1835008
  119.3 0.0 copy-done
  119.3 0.6 copy.14
Async XLA Ops:
  115.7 3.6 %copy-start = (f32[8,8]{1,0:T(8,128)S(1)}, f32[8,8]{1,0:T(8,128)}, u32[]{:S(2)}) copy-start(f32[8,8]{1,0:T(8,128)} %get-tuple-element.8) | copy-start | bytes 772

commit v2 on v1

--- a/solution.py
+++ b/solution.py
@@ -11,6 +11,7 @@
 F32 = jnp.float32
 BF16 = jnp.bfloat16
 LANES = 128
+LAG = 1
 VMEM_BYTES = 60 * 1024 * 1024
 
 
@@ -33,15 +34,19 @@
     R,
     sections,
     split,
-    x_ref,
-    g_ref,
-    ids_ref,
-    aff_ref,
+    x_hbm,
+    g_hbm,
+    ids_hbm,
+    aff_hbm,
     win_hbm,
     wout_hbm,
     dx_out,
     gd_out,
     sg_out,
+    x_ref,
+    g_ref,
+    ids_ref,
+    aff_ref,
     buf,
     win,
     wout,
@@ -115,21 +120,26 @@
 
     load_in = pltpu.make_async_copy(win_hbm, win, load_sem.at[0])
     load_out = pltpu.make_async_copy(wout_hbm, wout, load_sem.at[1])
+    loads = [
+        pltpu.make_async_copy(src, dst, load_sem.at[2 + i])
+        for i, (src, dst) in enumerate(((x_hbm, x_ref), (g_hbm, g_ref), (ids_hbm, ids_ref), (aff_hbm, aff_ref)))
+    ]
+    for load in loads:
+        load.start()
     load_in.start()
     load_out.start()
 
     barrier = pltpu.get_barrier_semaphore()
     source = wrap(sec - 1 + 2 * c, sections)
-    for device in (
-        a_next,
-        a_prev,
-        b_next,
-        b_prev,
-        sibling,
-        {"expert": chip * 2, "section": source},
-        {"expert": chip * 2 + 1, "section": source},
-    ):
+    peers = [a_next, a_prev, b_next, b_prev, sibling]
+    peers += [{"expert": chip * 2, "section": source}, {"expert": chip * 2 + 1, "section": source}]
+    if half > 1:
+        peers += [at(wrap(a + 2, R), b), at(wrap(a - 2, R), b)]
+    for device in peers:
         pl.semaphore_signal(barrier, inc=1, device_id=device, device_id_type=MESH)
+
+    for load in loads:
+        load.wait()
 
     def packed(value):
         wide = value.astype(F32)
@@ -146,7 +156,7 @@
     for k in range(top):
         dense = dense + jnp.where(lane8 == ids[:, k : k + 1], weight[:, k : k + 1], 0.0)
     wt_src[...] = dense
-    pl.semaphore_wait(barrier, 7)
+    pl.semaphore_wait(barrier, len(peers))
 
     send_x = remote(
         shift_src.at[0], shift_dst.at[c], shift_send.at[0], shift_recv.at[c], {"expert": chip * 2, "section": sec_next}
@@ -186,51 +196,71 @@
     def to_sibling(origin, j):
         return remote(buf.at[c, origin, j], buf.at[c, origin, j], sib_send.at[origin], sib_recv.at[origin], sibling)
 
-    for o in range(R):
+    def first_hop(o):
         hops, sign = order_of(R - 1 - o, R)
         j = wrap(a + sign * hops, R)
-        if o == 0:
+
+        @pl.when(o == 0)
+        def _():
             if half > 1:
                 along_a(j, 0, 1).start()
             along_a(j, 1, 1).start()
-        elif sign > 0:
+
+        @pl.when(jnp.logical_and(o > 0, sign > 0))
+        def _():
             along_a(j, 1, hops).wait_recv()
-            if hops < half:
+
+            @pl.when(hops < half)
+            def _():
                 along_a(j, 1, hops + 1).start()
+
+        @pl.when(jnp.logical_and(o > 0, sign < 0))
+        def _():
+            along_a(j, 0, hops).wait_recv()
+
+            @pl.when(hops < half - 1)
+            def _():
+                along_a(j, 0, hops + 1).start()
+
+        start_b(b, b, j, 1, o)
+        to_sibling(b, j).start()
+
+    def start_b(left, right, j, hop, o):
+        even = lax.rem(o, 2) == 0
+        if hop < half:
+            along_b(left, j, 0, hop, o).start()
+            along_b(right, j, 1, hop, o).start()
         else:
-            along_a(j, 0, hops).wait_recv()
-            if hops < half - 1:
-                along_a(j, 0, hops + 1).start()
-        if half > 1 or o < half:
-            along_b(b, j, 0, 1, o).start()
-        if half > 1 or o >= half:
-            along_b(b, j, 1, 1, o).start()
-        to_sibling(b, j).start()
-
-    def forward(hop, o, carry):
+
+            @pl.when(even)
+            def _():
+                along_b(left, j, 0, hop, o).start()
+
+            @pl.when(jnp.logical_not(even))
+            def _():
+                along_b(right, j, 1, hop, o).start()
+
+    def next_hop(hop, o):
         j = place(R - 1 - o, a, R)
         left, right = wrap(b - (hop - 1), R), wrap(b + (hop - 1), R)
-        along_b(left, j, 0, hop - 1, o).wait_recv()
-        if hop < half:
-            along_b(left, j, 0, hop, o).start()
+        if hop <= half:
+            along_b(left, j, 0, hop - 1, o).wait_recv()
+            along_b(right, j, 1, hop - 1, o).wait_recv()
+            start_b(left, right, j, hop, o)
+            to_sibling(left, j).start()
+            to_sibling(right, j).start()
         else:
-
-            @pl.when(o < half)
+            even = lax.rem(o, 2) == 0
+
+            @pl.when(even)
             def _():
-                along_b(left, j, 0, hop, o).start()
-
-        to_sibling(left, j).start()
-        along_b(right, j, 1, hop - 1, o).wait_recv()
-        if hop < half:
-            along_b(right, j, 1, hop, o).start()
-        else:
-
-            @pl.when(o >= half)
+                along_b(left, j, 0, half, o).wait_recv()
+
+            @pl.when(jnp.logical_not(even))
             def _():
-                along_b(right, j, 1, hop, o).start()
-
-        to_sibling(right, j).start()
-        return carry
+                along_b(left, j, 1, half, o).wait_recv()
+
+            to_sibling(left, j).start()
 
     def wait_sibling(origin):
         remote(buf.at[1 - c, origin], buf.at[1 - c, origin], sib_send.at[origin], sib_recv.at[origin], sibling).wait_recv()
@@ -246,41 +276,44 @@
         qb[:, y_slab] = q.reshape(R, block, units)
 
     def project_at(distance):
-        if distance == 0 or distance == half:
-            wait_sibling(wrap(a + distance, R))
-            project(wrap(z + distance, R), wrap(y + distance, R))
-        else:
-
-            def side(i, carry):
-                step = distance * (1 - 2 * i)
+        def side(i, carry):
+            step = distance * (1 - 2 * i)
+
+            @pl.when(jnp.logical_or(i == 0, jnp.logical_and(distance > 0, distance < half)))
+            def _():
                 wait_sibling(wrap(a + step, R))
                 project(wrap(z + step, R), wrap(y + step, R))
-                return carry
-
-            lax.fori_loop(0, 2, side, 0)
-
-    for hop in range(2, half + 1):
-        lax.fori_loop(0, R, functools.partial(forward, hop), 0)
-        if hop == 2:
+
+            return carry
+
+        lax.fori_loop(0, 2, side, 0)
+
+    def step(t, carry):
+        for hop in range(1, half + 2):
+            for i in range(2):
+                o = 2 * (t - LAG * (hop - 1)) - 1 + i
+
+                @pl.when(jnp.logical_and(o >= 0, o < R))
+                def _():
+                    if hop == 1:
+                        first_hop(o)
+                    else:
+                        next_hop(hop, o)
+
+        since = t - (half + 1)
+
+        @pl.when(since == 0)
+        def _():
             load_in.wait()
             load_out.wait()
-        project_at(hop - 2)
-    if half == 1:
-        load_in.wait()
-        load_out.wait()
-    project_at(half - 1)
-    far = wrap(b + half, R)
-
-    def last(o, carry):
-        j = place(R - 1 - o, a, R)
-        along_b(far, j, 0, half, o).wait_recv()
-        to_sibling(far, j).start()
-        j = place(R - 1 - (o + half), a, R)
-        along_b(far, j, 1, half, o + half).wait_recv()
-        to_sibling(far, j).start()
+
+        @pl.when(jnp.logical_and(since >= 0, lax.rem(since + LAG, LAG) == 0))
+        def _():
+            project_at(lax.div(since, LAG))
+
         return carry
 
-    lax.fori_loop(0, half, last, 0)
+    lax.fori_loop(0, half + LAG * half + 1, step, 0)
     project_at(half)
 
     def activate(z_slab, carry):
@@ -342,91 +375,93 @@
             parts.append(rb[zi, yi].astype(F32)[None])
         return jnp.concatenate(parts, axis=0)
 
-    def keep(n):
-        acc[...] = products(place(n, b, R), a, c, c).reshape(groups, per, block, H)
-        pair_copy(n).wait_recv()
-
-    def local_sum(n, g):
-        value = acc[g] + pair_dst[n, pl.ds(g * per, per)].astype(F32)
+    def keep(n, slot):
+        acc[slot] = products(place(n, b, R), a, c, c).reshape(groups, per, block, H)
+
+    def local_sum(n, slot, g):
+        value = acc[slot, g] + pair_dst[n, pl.ds(g * per, per)].astype(F32)
         return value, dense_r(place(n, b, R), g)
 
     def send_on(way, hop, g, value, r_value):
         ring_src[way, hop, g, :, :, 0:H] = value.astype(BF16)
         ring_src[way, hop, g, :, :, H:] = r_value.astype(BF16)
 
-    def start_ring(hop, g, sign):
-        @pl.when(sign > 0)
+    give(0)
+    keep(0, 0)
+    for i in range(1, min(R, 3)):
+        give(i)
+
+    pair_copy(0).wait_recv()
+    for i in range(groups // 2):
+        for way in range(2):
+            g = i + way * (groups // 2)
+            value, r_value = local_sum(0, 0, g)
+            send_on(way, half, g, value, r_value)
+            ring_copy(way, half, g).start()
+
+    def relay(partial, s, carry):
+        hops = half - s
+        for way in (1, 0):
+            keep(2 * s - way, way)
+        for way in (1, 0):
+            pair_copy(2 * s - way).wait_recv()
+
+        def group(g, carry):
+            for way in (1, 0):
+                n = 2 * s - way
+                value, r_value = local_sum(n, way, g)
+
+                def with_arrived():
+                    wait_ring(way, hops + 1, g)
+                    arrived = ring_dst[way, hops + 1, g].astype(F32)
+                    send_on(way, hops, g, value + arrived[:, :, 0:H], r_value + arrived[:, :, H:])
+
+                if partial:
+                    here = lax.div(g, groups // 2) == way
+
+                    @pl.when(here)
+                    def _():
+                        with_arrived()
+
+                    @pl.when(jnp.logical_not(here))
+                    def _():
+                        send_on(way, hops, g, value, r_value)
+
+                else:
+                    with_arrived()
+                ring_copy(way, hops, g).start()
+            return carry
+
+        lax.fori_loop(0, groups, group, 0)
+
+        @pl.when(2 * s + 1 < R)
         def _():
-            ring_copy(0, hop, g).start()
-
-        @pl.when(sign < 0)
+            give(2 * s + 1)
+
+        @pl.when(2 * s + 2 < R)
         def _():
-            ring_copy(1, hop, g).start()
-
-    give(0)
-    if R > 1:
-        give(1)
-
-    keep(0)
-    give(min(2, R - 1)) if R > 2 else None
-    for g in range(groups):
-        way = 0 if g < groups // 2 else 1
-        value, r_value = local_sum(0, g)
-        send_on(way, half, g, value, r_value)
-        ring_copy(way, half, g).start()
-
-    def relay(partial, n, carry):
-        hops, sign = order_of(n, R)
-        way = lax.rem(n, 2)
-        keep(n)
-
-        @pl.when(n + 2 < R)
-        def _():
-            give(n + 2)
-
-        def group(g, carry):
-            value, r_value = local_sum(n, g)
-
-            def with_arrived():
-                back = ring_dst.at[way, hops + 1, g]
-                remote(
-                    back, back, ring_send.at[way, hops + 1], ring_recv.at[way, hops + 1, g], sibling
-                ).wait_recv()
-                arrived = back[...].astype(F32)
-                send_on(way, hops, g, value + arrived[:, :, 0:H], r_value + arrived[:, :, H:])
-
-            if partial:
-                here = lax.div(g, groups // 2) == way
-
-                @pl.when(here)
-                def _():
-                    with_arrived()
-
-                @pl.when(jnp.logical_not(here))
-                def _():
-                    send_on(way, hops, g, value, r_value)
-
-            else:
-                with_arrived()
-            start_ring(hops, g, sign)
-            return carry
-
-        lax.fori_loop(0, groups, group, 0)
+            give(2 * s + 2)
+
         return carry
 
     if R > 2:
-        lax.fori_loop(1, 3, functools.partial(relay, True), 0)
+        relay(True, 1, 0)
     if R > 4:
-        lax.fori_loop(3, R - 1, functools.partial(relay, False), 0)
-
-    def line_copy(way, hop):
+        lax.fori_loop(2, half, functools.partial(relay, False), 0)
+
+    def line_copy(u):
+        hops, sign = order_of(u, R)
+        reach = hops if hops <= 2 else hops - 2
         return remote(
-            line_src.at[way, hop],
-            line_dst.at[way, hop],
-            line_send.at[way, hop],
-            line_recv.at[way, hop],
-            a_next if way == 0 else a_prev,
+            line_src.at[u], line_dst.at[u], line_send.at[u], line_recv.at[u], at(wrap(a + sign * reach, R), b)
         )
+
+    def senders(hops, signs):
+        found = []
+        for u in range(R - 1):
+            if order_of(u, R)[0] in hops and order_of(u, R)[1] in signs:
+                found.append(u)
+        return found
 
     chunk = D // 7 if D % (7 * LANES) == 0 else LANES
     chunks = D // chunk
@@ -440,10 +475,11 @@
         ).astype(BF16)
 
     n = R - 1
-    keep(n)
+    keep(n, 0)
+    pair_copy(n).wait_recv()
     done = 0
     for g in range(groups):
-        value, r_value = local_sum(n, g)
+        value, r_value = local_sum(n, 0, g)
         for way in range(2):
             if half > 1 or (g < groups // 2) == (way == 0):
                 wait_ring(way, 1, g)
@@ -454,21 +490,25 @@
             u = g * per + i
             hops, sign = order_of(u, R)
             v, rv = value[i], r_value[i]
-            while done < chunks and done < (u + 1) * chunks // R:
-                grad_down(done)
-                done += 1
-            ways = (0, 1) if hops == 0 else ((0,) if sign > 0 else (1,))
-            for way in ways:
-                if hops + 1 <= (half if way == 0 else half - 1):
-                    line_copy(way, hops + 1).wait_recv()
-                    arrived = line_dst[way, hops + 1].astype(F32)
-                    v = v + arrived[:, 0:H]
-                    rv = rv + arrived[:, H:]
+            arriving = []
+            if hops == 2:
+                arriving = senders((3, 4), (sign,))
+            elif hops == 0:
+                arriving = senders((1, 2), (1, -1))
+            if arriving:
+                stop = chunks if hops == 0 else min(chunks, done + 2)
+                while done < stop:
+                    grad_down(done)
+                    done += 1
+            for other in arriving:
+                line_copy(other).wait_recv()
+                arrived = line_dst[other].astype(F32)
+                v = v + arrived[:, 0:H]
+                rv = rv + arrived[:, H:]
             if hops > 0:
-                way = ways[0]
-                line_src[way, hops, :, 0:H] = v.astype(BF16)
-                line_src[way, hops, :, H:] = rv.astype(BF16)
-                line_copy(way, hops).start()
+                line_src[u, :, 0:H] = v.astype(BF16)
+                line_src[u, :, H:] = rv.astype(BF16)
+                line_copy(u).start()
             else:
                 fin_src[:, 0:H] = jnp.where(c == 0, v[rows:], v[:rows])
                 fin_src[:, H:] = jnp.where(c == 0, rv[rows:], rv[:rows])
@@ -504,9 +544,9 @@
             parts = groups if hop < half else groups // 2
             sent = ring_src.at[way, hop, pl.ds(0, parts)]
             remote(sent, sent, ring_send.at[way, hop], ring_recv.at[way, hop, 0], sibling).wait_send()
-        line_copy(0, hop).wait_send()
-        if hop < half:
-            line_copy(1, hop).wait_send()
+
+    for u in range(R - 1):
+        line_copy(u).wait_send()
 
     def settle(i, carry):
         remote(buf.at[c, i], buf.at[c, i], sib_send.at[i], sib_recv.at[i], sibling).wait_send()
@@ -537,7 +577,7 @@
     per = max(1, R // 4)
     groups = R // per
     vmem = pl.BlockSpec(memory_space=pltpu.VMEM)
-    anywhere = pl.BlockSpec(memory_space=pl.ANY)
+    hbm = pl.BlockSpec(memory_space=pltpu.HBM)
     dma = pltpu.SemaphoreType.DMA
     flops = 2 * slices * rows * D * units * 6
     dx, gd, sg = pl.pallas_call(
@@ -547,9 +587,13 @@
             jax.ShapeDtypeStruct((units, D), BF16),
             jax.ShapeDtypeStruct((rows, top), F32),
         ),
-        in_specs=[vmem, vmem, vmem, vmem, anywhere, anywhere],
+        in_specs=[hbm] * 6,
         out_specs=(vmem, vmem, vmem),
         scratch_shapes=[
+            pltpu.VMEM((rows, D), BF16),
+            pltpu.VMEM((rows, D), BF16),
+            pltpu.VMEM((rows, top), jnp.int32),
+            pltpu.VMEM((rows, top), F32),
             pltpu.VMEM((2, R, R, block, D + LANES), BF16),
             pltpu.VMEM((2, H, 2 * units), BF16),
             pltpu.VMEM((units, D), BF16),
@@ -562,16 +606,16 @@
             pltpu.VMEM((R, R, block, 2 * units), BF16),
             pltpu.VMEM((R, R, block, units), BF16),
             pltpu.VMEM((R, R, block, LANES), BF16),
-            pltpu.VMEM((groups, per, block, H), F32),
+            pltpu.VMEM((2, groups, per, block, H), F32),
             pltpu.VMEM((R, R, block, H), BF16),
             pltpu.VMEM((R, R, block, H), BF16),
             pltpu.VMEM((2, half + 1, groups, per, block, H + LANES), BF16),
             pltpu.VMEM((2, half + 1, groups, per, block, H + LANES), BF16),
-            pltpu.VMEM((2, half + 1, block, H + LANES), BF16),
-            pltpu.VMEM((2, half + 1, block, H + LANES), BF16),
+            pltpu.VMEM((R, block, H + LANES), BF16),
+            pltpu.VMEM((R, block, H + LANES), BF16),
             pltpu.VMEM((rows, H + LANES), F32),
             pltpu.VMEM((rows, H + LANES), F32),
-            dma((2,)),
+            dma((6,)),
             dma((2,)),
             dma((2,)),
             dma((2,)),
@@ -585,8 +629,8 @@
             dma((R,)),
             dma((2, half + 1)),
             dma((2, half + 1, groups)),
-            dma((2, half + 1)),
-            dma((2, half + 1)),
+            dma((R,)),
+            dma((R,)),
             dma((2,)),
         ],
         compiler_params=pltpu.CompilerParams(

time: 120 us -> 109 us (0.908)
  Pallas kernels: 115 us -> 104 us
    pallas_call x1, Pallas kernels: 115 us -> 104 us  [on_device(): pl.pallas_call(functools.partial(kernel, R, sections, split), out_shape=(...]
where the time goes in v2:
time: 109 us
  Pallas kernels  104 us (95%)
  local copies, waits for them, and re-layouts  4.2 us (4%)
    pallas_call x1, Pallas kernels, on_device(): pl.pallas_call(functools.partial(kernel, R, sections, split), out_shape=(...  104 us
    unnamed x5, local copies, waits for them, and re-layouts  4.2 us

profile of v2, /device:TPU:1, one launch (start us, length us, event | category | flops | bytes accessed | tf_op | source)
XLA Modules:
  0.0 109.2 jit_solution(8697047609449404725)
XLA Ops:
  0.6 104.3 %shard_map.85 = (bf16[8,3584]{1,0:T(8,128)(2,1)}, bf16[128,3584]{1,0:T(8,128)(2,1)}, f32[8,8]{1,0:T(8,128)}) custom-call(bf16[8,3584]{1,0:T(8,128)(2,1)} %bitcast.14, bf16[8,3584]{1,0:T(8,128)(2,1)} %bitcast.15, s32[8,8]{1,0:T(8,128)} %bitcast.16, f32[8,8]{1,0:T(8,128)} %bitcast.17, bf16[2,1792,256]{2,1,0:T(8,128)(2,1)} %bitcast.12, bf16[128,3584]{1,0:T(8,128)(2,1)} %bitcast.13), custom_call_target="tpu_custom_call" | custom-call | flops 5637144576 | bytes 3670016 | tf_op jit(solution)/shard_map/pallas_call | solution.py:583
  105.0 0.0 copy-start
  105.0 1.4 %copy.12 = bf16[1,8,3584]{2,1,0:T(8,128)(2,1)} copy(bf16[1,8,3584]{2,1,0:T(8,128)(2,1)} %bitcast.10) | data formatting | bytes 114688
  106.4 2.2 %copy.13 = bf16[1,1,128,3584]{3,2,1,0:T(8,128)(2,1)} copy(bf16[1,1,128,3584]{3,2,1,0:T(8,128)(2,1)} %bitcast.9) | data formatting | bytes 1835008
  108.6 0.0 copy-done
  108.6 0.6 copy.14
Async XLA Ops:
  105.0 3.6 %copy-start = (f32[8,8]{1,0:T(8,128)S(1)}, f32[8,8]{1,0:T(8,128)}, u32[]{:S(2)}) copy-start(f32[8,8]{1,0:T(8,128)} %get-tuple-element.8) | copy-start | bytes 772

commit v3 on v2

--- a/solution.py
+++ b/solution.py
@@ -56,6 +56,7 @@
     wt_dst,
     ab,
     qb,
+    wl,
     gab,
     hw,
     rb,
@@ -268,12 +269,14 @@
     def project(z_slab, y_slab):
         rows_lo = buf[0, z_slab, :, :, 0:H].reshape(R * block, H)
         rows_hi = buf[0, z_slab, :, :, H:D].reshape(R * block, H)
-        ab[z_slab] = jnp.dot(rows_lo, win[0], preferred_element_type=F32) + jnp.dot(
+        value = jnp.dot(rows_lo, win[0], preferred_element_type=F32) + jnp.dot(
             rows_hi, win[1], preferred_element_type=F32
         )
+        ab[z_slab] = value.reshape(R, block, 2 * units)
         rows_g = buf[1, y_slab, :, :, 0:D].reshape(R * block, D)
         q = lax.dot_general(rows_g, wout[...], (((1,), (1,)), ((), ())), preferred_element_type=F32)
         qb[:, y_slab] = q.reshape(R, block, units)
+        wl[:, y_slab] = buf[1, y_slab, :, :, D:]
 
     def project_at(distance):
         def side(i, carry):
@@ -288,7 +291,26 @@
 
         lax.fori_loop(0, 2, side, 0)
 
-    def step(t, carry):
+    def activate(z_at, y_at):
+        tall = R * block
+        lane = lax.broadcasted_iota(jnp.int32, (tall, LANES), 1)
+        wt = buf[0, z_at, y_at, :, D:].astype(F32) + wl[z_at, y_at].astype(F32)
+        w = jnp.sum(jnp.where(lane == expert, wt.reshape(tall, LANES), 0.0), axis=1, keepdims=True)
+        a_part = ab[z_at, y_at, :, 0:units].reshape(tall, units)
+        b_part = ab[z_at, y_at, :, units:].reshape(tall, units)
+        q = qb[z_at, y_at].reshape(tall, units) * w
+        sig = jax.nn.sigmoid(a_part)
+        active = a_part * sig
+        hidden = active * b_part
+        r = jnp.sum(hidden.astype(BF16).astype(F32) * q, axis=1, keepdims=True)
+        gab[z_at, y_at, :, 0:units] = (
+            (q * b_part * sig * (1.0 + a_part * (1.0 - sig))).astype(BF16).reshape(R, block, units)
+        )
+        gab[z_at, y_at, :, units:] = (q * active).astype(BF16).reshape(R, block, units)
+        hw[y_at, z_at] = (hidden * w).astype(BF16).reshape(R, block, units)
+        rb[z_at, y_at] = jnp.where(lane == expert, r, 0.0).astype(BF16).reshape(R, block, LANES)
+
+    def forward_at(t):
         for hop in range(1, half + 2):
             for i in range(2):
                 o = 2 * (t - LAG * (hop - 1)) - 1 + i
@@ -300,6 +322,8 @@
                     else:
                         next_hop(hop, o)
 
+    def step(t, carry):
+        forward_at(t)
         since = t - (half + 1)
 
         @pl.when(since == 0)
@@ -313,29 +337,26 @@
 
         return carry
 
-    lax.fori_loop(0, half + LAG * half + 1, step, 0)
+    final = half + LAG * half
+    lax.fori_loop(0, final, step, 0)
+    if half == 1:
+        load_in.wait()
+        load_out.wait()
+    project_at(half - 1)
+    z_far, y_far = wrap(z + half, R), wrap(y + half, R)
+    qb[:, y_far] = jnp.zeros((R, block, units), F32)
+    wl[:, y_far] = jnp.zeros((R, block, LANES), BF16)
+
+    def near(i, carry):
+        activate(wrap(z_far + 1 + i, R), slice(None))
+        return carry
+
+    lax.fori_loop(0, R - 1, near, 0)
+    forward_at(final)
     project_at(half)
-
-    def activate(z_slab, carry):
-        lane = lax.broadcasted_iota(jnp.int32, (R * block, LANES), 1)
-        wt = buf[0, z_slab, :, :, D:].astype(F32) + buf[1, :, z_slab, :, D:].astype(F32)
-        w = jnp.sum(jnp.where(lane == expert, wt.reshape(R * block, LANES), 0.0), axis=1, keepdims=True)
-        a_part = ab[z_slab, :, 0:units]
-        b_part = ab[z_slab, :, units:]
-        q = qb[z_slab].reshape(R * block, units) * w
-        sig = jax.nn.sigmoid(a_part)
-        active = a_part * sig
-        hidden = active * b_part
-        r = jnp.sum(hidden.astype(BF16).astype(F32) * q, axis=1, keepdims=True)
-        gab[z_slab, :, :, 0:units] = (
-            (q * b_part * sig * (1.0 + a_part * (1.0 - sig))).astype(BF16).reshape(R, block, units)
-        )
-        gab[z_slab, :, :, units:] = (q * active).astype(BF16).reshape(R, block, units)
-        hw[:, z_slab] = (hidden * w).astype(BF16).reshape(R, block, units)
-        rb[z_slab] = jnp.where(lane == expert, r, 0.0).astype(BF16).reshape(R, block, LANES)
-        return carry
-
-    lax.fori_loop(0, R, activate, 0)
+    activate(z_far, slice(None))
+    activate(slice(None), y_far)
+
 
     def spot(target, j, swap):
         return target + swap * (j - target), j + swap * (target - j)
@@ -388,8 +409,7 @@
 
     give(0)
     keep(0, 0)
-    for i in range(1, min(R, 3)):
-        give(i)
+    give(1)
 
     pair_copy(0).wait_recv()
     for i in range(groups // 2):
@@ -398,6 +418,8 @@
             value, r_value = local_sum(0, 0, g)
             send_on(way, half, g, value, r_value)
             ring_copy(way, half, g).start()
+    if R > 2:
+        give(2)
 
     def relay(partial, s, carry):
         hops = half - s
@@ -556,6 +578,20 @@
     lax.fori_loop(0, R, settle, 0)
 
 
+def finish(dx_in, gd_in, sg_in, dx_out, gd_out, sg_out, dx_mid, gd_mid, sg_mid, sem):
+    into = ((dx_in, dx_mid), (gd_in, gd_mid), (sg_in, sg_mid))
+    out = ((dx_mid, dx_out), (gd_mid, gd_out), (sg_mid, sg_out))
+    loads = [pltpu.make_async_copy(src, dst, sem.at[0, i]) for i, (src, dst) in enumerate(into)]
+    stores = [pltpu.make_async_copy(src, dst, sem.at[1, i]) for i, (src, dst) in enumerate(out)]
+    for load in loads:
+        load.start()
+    for load, store in zip(loads, stores):
+        load.wait()
+        store.start()
+    for store in stores:
+        store.wait()
+
+
 def side_of(devices):
     R = 1
     while 2 * R * R < devices:
@@ -601,8 +637,9 @@
             pltpu.VMEM((2, block, H), BF16),
             pltpu.VMEM((rows, LANES), F32),
             pltpu.VMEM((rows, LANES), F32),
-            pltpu.VMEM((R, R * block, 2 * units), F32),
+            pltpu.VMEM((R, R, block, 2 * units), F32),
             pltpu.VMEM((R, R, block, units), F32),
+            pltpu.VMEM((R, R, block, LANES), BF16),
             pltpu.VMEM((R, R, block, 2 * units), BF16),
             pltpu.VMEM((R, R, block, units), BF16),
             pltpu.VMEM((R, R, block, LANES), BF16),
@@ -645,6 +682,19 @@
         w_gate_up[0, 0].reshape(2, H, 2 * units),
         w_down[0, 0],
     )
+    dx, gd, sg = pl.pallas_call(
+        finish,
+        out_shape=(
+            jax.ShapeDtypeStruct((rows, D), BF16),
+            jax.ShapeDtypeStruct((units, D), BF16),
+            jax.ShapeDtypeStruct((rows, top), F32),
+        ),
+        in_specs=[hbm] * 3,
+        out_specs=(hbm,) * 3,
+        scratch_shapes=[pltpu.VMEM((rows, D), BF16), pltpu.VMEM((units, D), BF16), pltpu.VMEM((rows, top), F32), dma((2, 3))],
+        compiler_params=pltpu.CompilerParams(vmem_limit_bytes=VMEM_BYTES),
+        cost_estimate=pl.CostEstimate(flops=0, bytes_accessed=4 * D * (units + rows), transcendentals=0),
+    )(dx, gd, sg)
     return dx[None], gd[None, None], sg[None]
 
 

time: 109 us -> 106 us (0.972)
  local copies, waits for them, and re-layouts: 4.2 us -> 0 us
    unnamed x5 -> x0, local copies, waits for them, and re-layouts: 4.2 us -> none
    pallas_call x0 -> x1, Pallas kernels: none -> 2.19 us  [on_device(): pl.pallas_call(finish, out_shape=(jax.ShapeDtypeStruct((rows, D), BF16),...]
    pallas_call x1, Pallas kernels: 104 us -> 103 us  [on_device(): pl.pallas_call(functools.partial(kernel, R, sections, split), out_shape=(...]
where the time goes in v3:
time: 106 us
  Pallas kernels  105 us (99%)
    pallas_call x1, Pallas kernels, on_device(): pl.pallas_call(functools.partial(kernel, R, sections, split), out_shape=(...  103 us
    pallas_call x1, Pallas kernels, on_device(): pl.pallas_call(finish, out_shape=(jax.ShapeDtypeStruct((rows, D), BF16),...  2.19 us

profile of v3, /device:TPU:1, one launch (start us, length us, event | category | flops | bytes accessed | tf_op | source)
XLA Modules:
  0.0 105.9 jit_solution(18206501687281948053)
XLA Ops:
  0.6 103.1 %shard_map.85 = (bf16[8,3584]{1,0:T(8,128)(2,1)}, bf16[128,3584]{1,0:T(8,128)(2,1)}, f32[8,8]{1,0:T(8,128)}) custom-call(bf16[8,3584]{1,0:T(8,128)(2,1)} %bitcast.12, bf16[8,3584]{1,0:T(8,128)(2,1)} %bitcast.13, s32[8,8]{1,0:T(8,128)} %bitcast.15, f32[8,8]{1,0:T(8,128)} %bitcast.16, bf16[2,1792,256]{2,1,0:T(8,128)(2,1)} %bitcast.9, bf16[128,3584]{1,0:T(8,128)(2,1)} %bitcast.10), custom_call_target="tpu_custom_call" | custom-call | flops 5637144576 | bytes 3670016 | tf_op jit(solution)/shard_map/pallas_call | solution.py:619
  103.7 2.2 %shard_map.86 = (bf16[8,3584]{1,0:T(8,128)(2,1)}, bf16[128,3584]{1,0:T(8,128)(2,1)}, f32[8,8]{1,0:T(8,128)}) custom-call(bf16[8,3584]{1,0:T(8,128)(2,1)} %get-tuple-element.9.dx_in, bf16[128,3584]{1,0:T(8,128)(2,1)} %get-tuple-element.10.gd_in, f32[8,8]{1,0:T(8,128)} %get-tuple-element.11.sg_in), custom_call_target="tpu_custom_call" | custom-call | bytes 1949696 | tf_op jit(solution)/shard_map/pallas_call | solution.py:685

commit v4 on v3

--- a/solution.py
+++ b/solution.py
@@ -180,10 +180,15 @@
     buf[c, b, a, :, H:D] = jnp.concatenate([low[rows:], high[rows:]], axis=0).astype(BF16)
     buf[c, b, a, :, D:] = jnp.where(c == 0, lead, pair_wt - lead).astype(BF16)
 
-    def along_a(j, way, hop):
-        return remote(
-            buf.at[c, b, j], buf.at[c, b, j], a_send.at[way, hop], a_recv.at[way, hop], a_next if way == 0 else a_prev
-        )
+    def along_a(j, way, hop, reach=1):
+        device = at(wrap(a + (reach if way == 0 else -reach), R), b)
+        return remote(buf.at[c, b, j], buf.at[c, b, j], a_send.at[way, hop], a_recv.at[way, hop], device)
+
+    def start_a(j, base):
+        for reach in (1, 2):
+            for way in range(2):
+                if base + reach <= (half - 1 if way == 0 else half):
+                    along_a(j, way, base + reach, reach).start()
 
     def along_b(origin, j, way, hop, piece):
         return remote(
@@ -197,31 +202,30 @@
     def to_sibling(origin, j):
         return remote(buf.at[c, origin, j], buf.at[c, origin, j], sib_send.at[origin], sib_recv.at[origin], sibling)
 
+    def relay_a(j, way, hops):
+        @pl.when(hops == 2)
+        def _():
+            for reach in (1, 2):
+                if 2 + reach <= (half - 1 if way == 0 else half):
+                    along_a(j, way, 2 + reach, reach).start()
+
     def first_hop(o):
         hops, sign = order_of(R - 1 - o, R)
         j = wrap(a + sign * hops, R)
 
         @pl.when(o == 0)
         def _():
-            if half > 1:
-                along_a(j, 0, 1).start()
-            along_a(j, 1, 1).start()
+            start_a(j, 0)
 
         @pl.when(jnp.logical_and(o > 0, sign > 0))
         def _():
             along_a(j, 1, hops).wait_recv()
-
-            @pl.when(hops < half)
-            def _():
-                along_a(j, 1, hops + 1).start()
+            relay_a(j, 1, hops)
 
         @pl.when(jnp.logical_and(o > 0, sign < 0))
         def _():
             along_a(j, 0, hops).wait_recv()
-
-            @pl.when(hops < half - 1)
-            def _():
-                along_a(j, 0, hops + 1).start()
+            relay_a(j, 0, hops)
 
         start_b(b, b, j, 1, o)
         to_sibling(b, j).start()

time: 106 us -> 107 us (level)
  no operation moved by 1% of the time
where the time goes in v4:
time: 107 us; the launch traced here: 106 us
  Pallas kernels  106 us (99%)
    pallas_call x1, Pallas kernels, on_device(): pl.pallas_call(functools.partial(kernel, R, sections, split), out_shape=(...  104 us
    pallas_call x1, Pallas kernels, on_device(): pl.pallas_call(finish, out_shape=(jax.ShapeDtypeStruct((rows, D), BF16),...  2.19 us

profile of v4, /device:TPU:1, one launch (start us, length us, event | category | flops | bytes accessed | tf_op | source)
XLA Modules:
  0.0 106.5 jit_solution(17091625233027298396)
XLA Ops:
  0.6 103.6 %shard_map.85 = (bf16[8,3584]{1,0:T(8,128)(2,1)}, bf16[128,3584]{1,0:T(8,128)(2,1)}, f32[8,8]{1,0:T(8,128)}) custom-call(bf16[8,3584]{1,0:T(8,128)(2,1)} %bitcast.12, bf16[8,3584]{1,0:T(8,128)(2,1)} %bitcast.13, s32[8,8]{1,0:T(8,128)} %bitcast.15, f32[8,8]{1,0:T(8,128)} %bitcast.16, bf16[2,1792,256]{2,1,0:T(8,128)(2,1)} %bitcast.9, bf16[128,3584]{1,0:T(8,128)(2,1)} %bitcast.10), custom_call_target="tpu_custom_call" | custom-call | flops 5637144576 | bytes 3670016 | tf_op jit(solution)/shard_map/pallas_call | solution.py:623
  104.3 2.2 %shard_map.86 = (bf16[8,3584]{1,0:T(8,128)(2,1)}, bf16[128,3584]{1,0:T(8,128)(2,1)}, f32[8,8]{1,0:T(8,128)}) custom-call(bf16[8,3584]{1,0:T(8,128)(2,1)} %get-tuple-element.9.dx_in, bf16[128,3584]{1,0:T(8,128)(2,1)} %get-tuple-element.10.gd_in, f32[8,8]{1,0:T(8,128)} %get-tuple-element.11.sg_in), custom_call_target="tpu_custom_call" | custom-call | bytes 1949696 | tf_op jit(solution)/shard_map/pallas_call | solution.py:689
